TPU v7x, 256 devices: a whole 4x4x8 slice. The times are simulated.
256 devices in a mesh: dp: 128 (over z, x, y), pair: 2 (over core).
Axes of the slice: x: 4, y: 4, z: 8, core: 2. Of those that a mesh axis runs over, the one named last changes fastest.
Arguments:
- hidden_in: bfloat16 [32768, 1536], P(('dp', 'pair')), may hold values from -24 to 24
- segment_ids: int32 [32768], replicated, may hold values from 0 to 511, as said below
- frame_mask: int32 [32768], P(('dp', 'pair')), may hold values from 0 to 1, as said below
- dw_kernel: float32 [31, 1536], P(None, ('dp', 'pair')), may hold values from -1 to 1
- norm_scale: float32 [1536], P(('dp', 'pair')), may hold values from 0.1 to 1.9
- norm_shift: float32 [1536], P(('dp', 'pair')), may hold values from -3 to 3
- out_weight: bfloat16 [1536, 1536], P(('dp', 'pair')), may hold values from -0.15625 to 0.15625
- cotangent: bfloat16 [32768, 1536], P(('dp', 'pair')), may hold values from -6 to 6
Outputs:
- module_out: bfloat16 [32768, 1536], P(('dp', 'pair'))
- grad_hidden: bfloat16 [32768, 1536], P(('dp', 'pair'))
- grad_kernel: float32 [31, 1536], P(None, ('dp', 'pair'))
- grad_scale: float32 [1536], P(('dp', 'pair'))
- grad_shift: float32 [1536], P(('dp', 'pair'))
- grad_weight: float32 [1536, 1536], P(('dp', 'pair'))
Inputs may be any that keep to these rules, and one draw needn't show every extreme that they name: `segment_ids`: non-falling along the stream, starting at 0; each utterance has 1 to 192 frames; no utterance begins at a frame whose index is a positive multiple of 128. `frame_mask`: 1 on every frame whose index modulo 16 is 0 or 15.
All inputs are finite; a program needn't handle non-finite values.
Results may differ from a plain program's by a relative error of at most 0.0049.
Values may be sent and summed in bfloat16 or wider, within the bound.
No kernel may reach another device: no remote copies, remote signals or barrier semaphores. Data moves between devices by JAX's collectives and lax.ppermute only.
A program may use at most 128 MiB of HBM per device.

v0:
```python
import jax
import jax.numpy as jnp
from jax import lax
from jax.sharding import PartitionSpec as P

KERNEL = 31


def padded(cells, sides, width):
    for axis, dim in sides:
        count = lax.axis_size(axis)
        ends = count - 1
        head = lax.slice_in_dim(cells, 0, width, axis=dim)
        tail = lax.slice_in_dim(cells, cells.shape[dim] - width, cells.shape[dim], axis=dim)
        cells = jnp.concatenate(
            [
                lax.ppermute(tail, axis, [(i, (i + 1) % count) for i in range(ends)]),
                cells,
                lax.ppermute(head, axis, [((i + 1) % count, i) for i in range(ends)]),
            ],
            axis=dim,
        )
    return cells


def local(
    hidden_in, segment_ids, frame_mask, dw_kernel, norm_scale, norm_shift, out_weight, cotangent
):
    local_rows = hidden_in.shape[0]
    shard_cols = norm_scale.shape[0]
    half = KERNEL // 2
    device_pos = lax.axis_index(("dp", "pair"))
    weight_col = frame_mask.astype(jnp.float32)[:, None]
    stacked = jnp.concatenate([dw_kernel, norm_scale[None, :], norm_shift[None, :]], axis=0)
    params_full = lax.all_gather(stacked, ("dp", "pair"), axis=1, tiled=True)
    kernel_full = params_full[:KERNEL]
    scale_full = params_full[KERNEL]
    shift_full = params_full[KERNEL + 1]
    seg_pad = jnp.pad(segment_ids, (half, half), constant_values=-1)
    seg_local = lax.dynamic_slice_in_dim(seg_pad, device_pos * local_rows, local_rows + 2 * half)
    own_seg = seg_local[half : half + local_rows]
    masked = jnp.where(frame_mask[:, None] == 1, hidden_in, jnp.zeros_like(hidden_in))
    padded_in = padded(masked, ((("dp", "pair"), 0),), half).astype(jnp.float32)
    conv = jnp.zeros((local_rows, params_full.shape[1]), jnp.float32)
    for offset in range(KERNEL):
        same_seg = (seg_local[offset : offset + local_rows] == own_seg)[:, None]
        conv = conv + jnp.where(
            same_seg, kernel_full[offset] * padded_in[offset : offset + local_rows], 0.0
        )
    total, count = lax.psum(
        (jnp.sum(weight_col * conv, axis=0), jnp.sum(weight_col)), ("dp", "pair")
    )
    mean = total / count
    centred = conv - mean
    spread = lax.psum(jnp.sum(weight_col * centred * centred, axis=0), ("dp", "pair"))
    variance = spread / count
    inv_std = lax.rsqrt(variance + 1e-05)
    normed = centred * inv_std
    pre = scale_full * normed + shift_full
    sig = jax.nn.sigmoid(pre)
    act = (weight_col * pre * sig).astype(jnp.bfloat16)
    weight_full = lax.all_gather(out_weight, ("dp", "pair"), axis=0, tiled=True)
    module_out = jnp.dot(act, weight_full, preferred_element_type=jnp.float32).astype(jnp.bfloat16)
    grad_act = lax.dot_general(
        cotangent, weight_full, (((1,), (1,)), ((), ())), preferred_element_type=jnp.float32
    )
    grad_pre = weight_col * grad_act * sig * (1.0 + pre * (1.0 - sig))
    scale_sum, shift_sum = lax.psum(
        (jnp.sum(grad_pre * normed, axis=0), jnp.sum(grad_pre, axis=0)), ("dp", "pair")
    )
    col_start = device_pos * shard_cols
    grad_scale = lax.dynamic_slice_in_dim(scale_sum, col_start, shard_cols)
    grad_shift = lax.dynamic_slice_in_dim(shift_sum, col_start, shard_cols)
    grad_conv = (
        weight_col
        * scale_full
        * inv_std
        * (grad_pre - shift_sum / count - normed * scale_sum / count)
    )
    grad_pad = padded(grad_conv, ((("dp", "pair"), 0),), half)
    grad_local = jnp.zeros_like(grad_conv)
    tap_rows = []
    for offset in range(KERNEL):
        same_fwd = (seg_local[offset : offset + local_rows] == own_seg)[:, None]
        tap_rows.append(
            jnp.sum(
                jnp.where(same_fwd, grad_conv * padded_in[offset : offset + local_rows], 0.0),
                axis=0,
            )
        )
        back = 2 * half - offset
        same_back = (seg_local[back : back + local_rows] == own_seg)[:, None]
        grad_local = grad_local + jnp.where(
            same_back, kernel_full[offset] * grad_pad[back : back + local_rows], 0.0
        )
    grad_kernel = lax.psum_scatter(
        jnp.stack(tap_rows, axis=0), ("dp", "pair"), scatter_dimension=1, tiled=True
    )
    grad_hidden = (weight_col * grad_local).astype(jnp.bfloat16)
    grad_weight = lax.psum_scatter(
        lax.dot_general(
            act, cotangent, (((0,), (0,)), ((), ())), preferred_element_type=jnp.float32
        ),
        ("dp", "pair"),
        scatter_dimension=0,
        tiled=True,
    )
    return (module_out, grad_hidden, grad_kernel, grad_scale, grad_shift, grad_weight)


def solution(mesh):
    return jax.shard_map(
        local,
        mesh=mesh,
        in_specs=(
            P(("dp", "pair"), None),
            P(),
            P(("dp", "pair")),
            P(None, ("dp", "pair")),
            P(("dp", "pair")),
            P(("dp", "pair")),
            P(("dp", "pair"), None),
            P(("dp", "pair"), None),
        ),
        out_specs=(
            P(("dp", "pair"), None),
            P(("dp", "pair"), None),
            P(None, ("dp", "pair")),
            P(("dp", "pair")),
            P(("dp", "pair")),
            P(("dp", "pair"), None),
        ),
        check_vma=False,
    )
```

profile of v0, /device:TPU:1, one launch (start us, length us, event | category | flops | bytes accessed | tf_op | source)
XLA Modules:
  0.0 1933.7 jit_solution(4667449494425731221)
XLA Ops:
  19.3 68.0 %all-gather = f32[256,6,33]{2,1,0:T(8,128)S(1)} all-gather(f32[1,6,33]{2,1,0:T(8,128)S(1)} %maximum_bitcast_fusion), channel_id=1, replica_groups=mesh['dp'=128,'pair'=2] {'dp','pair'}, dimensions={0}, use_global_device_ids=true | all-gather | bytes 203544 | tf_op jit(solution)/shard_map/all_gather | solution.py:35
  107.4 75.7 %all-reduce.5 = (f32[1536]{0:T(1024)S(1)}, f32[]{:T(128)}) all-reduce(f32[1536]{0:T(1024)S(1)} %get-tuple-element.89, f32[]{:T(128)} %convert_reduce_fusion), channel_id=1, replica_groups=mesh['dp'=128,'pair'=2] {'dp','pair'}, use_global_device_ids=true, to_apply=%region_1.2 | all-reduce | flops 1537 | bytes 12296 | tf_op jit(solution)/shard_map/psum | solution.py:50
  184.0 74.2 %psum.37 = f32[1536]{0:T(1024)S(1)} all-reduce(f32[1536]{0:T(1024)S(1)} %fusion.119), channel_id=1, replica_groups=mesh['dp'=128,'pair'=2] {'dp','pair'}, use_global_device_ids=true, to_apply=%region_5.6 | all-reduce | flops 1536 | bytes 12288 | tf_op jit(solution)/shard_map/psum | solution.py:55
  264.0 709.9 %fusion = f32[8,1536]{1,0:T(8,128)S(1)} fusion(f32[1536,1536]{1,0:T(8,128)} %fusion.124), kind=kCustom, calls=%all-reduce-scatter | all-reduce-scatter fusion | flops 3145729 | bytes 9486336
  1005.7 17.9 collective-permute-start.51
  1066.6 13.1 collective-permute-start.34
  1079.7 13.1 collective-permute-start.33
  1092.9 13.1 collective-permute-start.32
  1106.0 13.1 collective-permute-start.31
  1119.2 13.1 collective-permute-start.30
  1132.3 13.1 collective-permute-start.29
  1145.5 13.1 collective-permute-start.28
  1158.6 13.1 collective-permute-start.27
  1171.8 13.1 collective-permute-start.26
  1184.9 13.1 collective-permute-start.25
  1198.1 13.1 collective-permute-start.24
  1211.2 13.1 collective-permute-start.23
  1224.4 13.1 collective-permute-start.22
  1237.5 13.1 collective-permute-start.21
  1250.7 13.1 collective-permute-start.20
  1263.8 13.1 collective-permute-start.19
  1277.0 13.1 collective-permute-start.18
  1290.1 13.1 collective-permute-start.17
  1303.3 13.1 collective-permute-start.16
  1316.4 13.3 collective-permute-start.15
  1408.6 13.7 collective-permute-start.8
  1422.4 13.1 collective-permute-start.7
  1435.5 13.1 collective-permute-start.6
  1448.7 13.1 collective-permute-start.5
  1466.0 97.2 %concatenate.45 = f32[518,1536]{1,0:T(8,128)} concatenate(f32[6,1536]{1,0:T(8,128)S(1)} %collective-permute-done.67, f32[8,1536]{1,0:T(8,128)S(1)} %collective-permute-done.66, f32[8,1536]{1,0:T(8,128)S(1)} %collective-permute-done.65, f32[8,1536]{1,0:T(8,128)S(1)} %collective-permute-done.64, f32[8,1536]{1,0:T(8,128)S(1)} %collective-permute-done.63, ...), dimensions={0} | concatenate | bytes 6365184
  1580.0 79.5 %all-reduce.4 = (f32[1536]{0:T(1024)S(1)}, f32[1536]{0:T(1024)S(1)}) all-reduce(f32[1536]{0:T(1024)S(1)} %get-tuple-element.50, f32[1536]{0:T(1024)S(1)} %get-tuple-element.49), channel_id=1, replica_groups=mesh['dp'=128,'pair'=2] {'dp','pair'}, use_global_device_ids=true, to_apply=%region_9.10 | all-reduce | flops 3072 | bytes 24576 | tf_op jit(solution)/shard_map/psum | solution.py:68
  1688.0 237.1 %all-reduce.8.cloned.1.call-done = f32[31,1536]{1,0:T(8,128)} async-done(((f32[31,1536]{1,0:T(8,128)}), f32[31,1536]{1,0:T(8,128)}) %all-reduce.8.cloned.1.call-update) | async-done | bytes 190480
  (362 shorter events, 241.3 us)
Async XLA Ops:
  7.2 1557.6 %all-gather.4.cloned.1.call-start = ((), (), s32[]{:S(2)}) async-start(), calls=%async_computation | async-start | bytes 6316032 | tf_op jit(solution)/shard_map/all_gather | solution.py:62
  7.9 1917.2 %all-reduce.8.cloned.1.call-start = ((), (), s32[]{:S(2)}) async-start(), calls=%async_computation.1 | async-start | bytes 393216
  9.7 92.7 %collective-permute-start = (bf16[15,1536]{1,0:T(8,128)(2,1)S(1)}, bf16[15,1536]{1,0:T(8,128)(2,1)S(1)}, u32[]{:S(2)}, u32[]{:S(2)}) collective-permute-start(bf16[15,1536]{1,0:T(8,128)(2,1)S(1)} %get-tuple-element.93), channel_id=1, source_target_pairs={{0,1},{1,2},{2,3},{3,4},{4,5},{5,6},{6,7},{7,8},{8,9},{9,10},{10,1... | collective-permute-start | bytes 138248 | tf_op jit(solution)/shard_map/ppermute | solution.py:17
  14.3 88.1 %collective-permute-start.1 = (bf16[15,1536]{1,0:T(8,128)(2,1)S(1)}, bf16[15,1536]{1,0:T(8,128)(2,1)S(1)}, u32[]{:S(2)}, u32[]{:S(2)}) collective-permute-start(bf16[15,1536]{1,0:T(8,128)(2,1)S(1)} %get-tuple-element.94), channel_id=1, source_target_pairs={{1,0},{2,1},{3,2},{4,3},{5,4},{6,5},{7,6},{8,7},{9,8},{10,9},{11,1... | collective-permute-start | bytes 138248 | tf_op jit(solution)/shard_map/ppermute | solution.py:19
  1060.5 58.7 %collective-permute-start.35 = (f32[8,1536]{1,0:T(8,128)S(1)}, f32[8,1536]{1,0:T(8,128)S(1)}, u32[]{:S(2)}, u32[]{:S(2)}) collective-permute-start(f32[8,1536]{1,0:T(8,128)S(1)} %fusion), channel_id=1, source_target_pairs={{0,32},{1,33},{2,34},{3,35},{4,36},{5,37},{6,38},{7,39},{8,40},{9,... | collective-permute-start | bytes 147464
  1066.6 65.7 %collective-permute-start.34 = (f32[8,1536]{1,0:T(8,128)S(1)}, f32[8,1536]{1,0:T(8,128)S(1)}, u32[]{:S(2)}, u32[]{:S(2)}) collective-permute-start(f32[8,1536]{1,0:T(8,128)S(1)} %fusion), channel_id=1, source_target_pairs={{0,31},{1,32},{2,33},{3,34},{4,35},{5,36},{6,37},{7,38},{8,39},{9,... | collective-permute-start | bytes 147464
  1079.7 65.7 %collective-permute-start.33 = (f32[8,1536]{1,0:T(8,128)S(1)}, f32[8,1536]{1,0:T(8,128)S(1)}, u32[]{:S(2)}, u32[]{:S(2)}) collective-permute-start(f32[8,1536]{1,0:T(8,128)S(1)} %fusion), channel_id=1, source_target_pairs={{0,30},{1,31},{2,32},{3,33},{4,34},{5,35},{6,36},{7,37},{8,38},{9,... | collective-permute-start | bytes 147464
  1092.9 65.7 %collective-permute-start.32 = (f32[8,1536]{1,0:T(8,128)S(1)}, f32[8,1536]{1,0:T(8,128)S(1)}, u32[]{:S(2)}, u32[]{:S(2)}) collective-permute-start(f32[8,1536]{1,0:T(8,128)S(1)} %fusion), channel_id=1, source_target_pairs={{0,29},{1,30},{2,31},{3,32},{4,33},{5,34},{6,35},{7,36},{8,37},{9,... | collective-permute-start | bytes 147464
  1106.0 65.7 %collective-permute-start.31 = (f32[8,1536]{1,0:T(8,128)S(1)}, f32[8,1536]{1,0:T(8,128)S(1)}, u32[]{:S(2)}, u32[]{:S(2)}) collective-permute-start(f32[8,1536]{1,0:T(8,128)S(1)} %fusion), channel_id=1, source_target_pairs={{0,28},{1,29},{2,30},{3,31},{4,32},{5,33},{6,34},{7,35},{8,36},{9,... | collective-permute-start | bytes 147464
  1119.2 65.7 %collective-permute-start.30 = (f32[8,1536]{1,0:T(8,128)S(1)}, f32[8,1536]{1,0:T(8,128)S(1)}, u32[]{:S(2)}, u32[]{:S(2)}) collective-permute-start(f32[8,1536]{1,0:T(8,128)S(1)} %fusion), channel_id=1, source_target_pairs={{0,27},{1,28},{2,29},{3,30},{4,31},{5,32},{6,33},{7,34},{8,35},{9,... | collective-permute-start | bytes 147464
  1132.3 65.7 %collective-permute-start.29 = (f32[8,1536]{1,0:T(8,128)S(1)}, f32[8,1536]{1,0:T(8,128)S(1)}, u32[]{:S(2)}, u32[]{:S(2)}) collective-permute-start(f32[8,1536]{1,0:T(8,128)S(1)} %fusion), channel_id=1, source_target_pairs={{0,26},{1,27},{2,28},{3,29},{4,30},{5,31},{6,32},{7,33},{8,34},{9,... | collective-permute-start | bytes 147464
  1145.5 65.7 %collective-permute-start.28 = (f32[8,1536]{1,0:T(8,128)S(1)}, f32[8,1536]{1,0:T(8,128)S(1)}, u32[]{:S(2)}, u32[]{:S(2)}) collective-permute-start(f32[8,1536]{1,0:T(8,128)S(1)} %fusion), channel_id=1, source_target_pairs={{0,25},{1,26},{2,27},{3,28},{4,29},{5,30},{6,31},{7,32},{8,33},{9,... | collective-permute-start | bytes 147464
  1158.6 65.7 %collective-permute-start.27 = (f32[8,1536]{1,0:T(8,128)S(1)}, f32[8,1536]{1,0:T(8,128)S(1)}, u32[]{:S(2)}, u32[]{:S(2)}) collective-permute-start(f32[8,1536]{1,0:T(8,128)S(1)} %fusion), channel_id=1, source_target_pairs={{0,24},{1,25},{2,26},{3,27},{4,28},{5,29},{6,30},{7,31},{8,32},{9,... | collective-permute-start | bytes 147464
  1171.8 65.7 %collective-permute-start.26 = (f32[8,1536]{1,0:T(8,128)S(1)}, f32[8,1536]{1,0:T(8,128)S(1)}, u32[]{:S(2)}, u32[]{:S(2)}) collective-permute-start(f32[8,1536]{1,0:T(8,128)S(1)} %fusion), channel_id=1, source_target_pairs={{0,23},{1,24},{2,25},{3,26},{4,27},{5,28},{6,29},{7,30},{8,31},{9,... | collective-permute-start | bytes 147464
  1184.9 65.7 %collective-permute-start.25 = (f32[8,1536]{1,0:T(8,128)S(1)}, f32[8,1536]{1,0:T(8,128)S(1)}, u32[]{:S(2)}, u32[]{:S(2)}) collective-permute-start(f32[8,1536]{1,0:T(8,128)S(1)} %fusion), channel_id=1, source_target_pairs={{0,22},{1,23},{2,24},{3,25},{4,26},{5,27},{6,28},{7,29},{8,30},{9,... | collective-permute-start | bytes 147464
  1198.1 65.7 %collective-permute-start.24 = (f32[8,1536]{1,0:T(8,128)S(1)}, f32[8,1536]{1,0:T(8,128)S(1)}, u32[]{:S(2)}, u32[]{:S(2)}) collective-permute-start(f32[8,1536]{1,0:T(8,128)S(1)} %fusion), channel_id=1, source_target_pairs={{0,21},{1,22},{2,23},{3,24},{4,25},{5,26},{6,27},{7,28},{8,29},{9,... | collective-permute-start | bytes 147464
  1211.2 65.7 %collective-permute-start.23 = (f32[8,1536]{1,0:T(8,128)S(1)}, f32[8,1536]{1,0:T(8,128)S(1)}, u32[]{:S(2)}, u32[]{:S(2)}) collective-permute-start(f32[8,1536]{1,0:T(8,128)S(1)} %fusion), channel_id=1, source_target_pairs={{0,20},{1,21},{2,22},{3,23},{4,24},{5,25},{6,26},{7,27},{8,28},{9,... | collective-permute-start | bytes 147464
  1224.4 65.7 %collective-permute-start.22 = (f32[8,1536]{1,0:T(8,128)S(1)}, f32[8,1536]{1,0:T(8,128)S(1)}, u32[]{:S(2)}, u32[]{:S(2)}) collective-permute-start(f32[8,1536]{1,0:T(8,128)S(1)} %fusion), channel_id=1, source_target_pairs={{0,19},{1,20},{2,21},{3,22},{4,23},{5,24},{6,25},{7,26},{8,27},{9,... | collective-permute-start | bytes 147464
  1237.5 65.7 %collective-permute-start.21 = (f32[8,1536]{1,0:T(8,128)S(1)}, f32[8,1536]{1,0:T(8,128)S(1)}, u32[]{:S(2)}, u32[]{:S(2)}) collective-permute-start(f32[8,1536]{1,0:T(8,128)S(1)} %fusion), channel_id=1, source_target_pairs={{0,18},{1,19},{2,20},{3,21},{4,22},{5,23},{6,24},{7,25},{8,26},{9,... | collective-permute-start | bytes 147464
  1250.7 65.7 %collective-permute-start.20 = (f32[8,1536]{1,0:T(8,128)S(1)}, f32[8,1536]{1,0:T(8,128)S(1)}, u32[]{:S(2)}, u32[]{:S(2)}) collective-permute-start(f32[8,1536]{1,0:T(8,128)S(1)} %fusion), channel_id=1, source_target_pairs={{0,17},{1,18},{2,19},{3,20},{4,21},{5,22},{6,23},{7,24},{8,25},{9,... | collective-permute-start | bytes 147464
  1263.8 65.9 %collective-permute-start.19 = (f32[8,1536]{1,0:T(8,128)S(1)}, f32[8,1536]{1,0:T(8,128)S(1)}, u32[]{:S(2)}, u32[]{:S(2)}) collective-permute-start(f32[8,1536]{1,0:T(8,128)S(1)} %fusion), channel_id=1, source_target_pairs={{0,16},{1,17},{2,18},{3,19},{4,20},{5,21},{6,22},{7,23},{8,24},{9,... | collective-permute-start | bytes 147464
  1277.0 65.9 %collective-permute-start.18 = (f32[8,1536]{1,0:T(8,128)S(1)}, f32[8,1536]{1,0:T(8,128)S(1)}, u32[]{:S(2)}, u32[]{:S(2)}) collective-permute-start(f32[8,1536]{1,0:T(8,128)S(1)} %fusion), channel_id=1, source_target_pairs={{0,15},{1,16},{2,17},{3,18},{4,19},{5,20},{6,21},{7,22},{8,23},{9,... | collective-permute-start | bytes 147464
  1290.1 65.9 %collective-permute-start.17 = (f32[8,1536]{1,0:T(8,128)S(1)}, f32[8,1536]{1,0:T(8,128)S(1)}, u32[]{:S(2)}, u32[]{:S(2)}) collective-permute-start(f32[8,1536]{1,0:T(8,128)S(1)} %fusion), channel_id=1, source_target_pairs={{0,14},{1,15},{2,16},{3,17},{4,18},{5,19},{6,20},{7,21},{8,22},{9,... | collective-permute-start | bytes 147464
  1303.3 65.9 %collective-permute-start.16 = (f32[8,1536]{1,0:T(8,128)S(1)}, f32[8,1536]{1,0:T(8,128)S(1)}, u32[]{:S(2)}, u32[]{:S(2)}) collective-permute-start(f32[8,1536]{1,0:T(8,128)S(1)} %fusion), channel_id=1, source_target_pairs={{0,13},{1,14},{2,15},{3,16},{4,17},{5,18},{6,19},{7,20},{8,21},{9,... | collective-permute-start | bytes 147464
  1316.4 65.9 %collective-permute-start.15 = (f32[8,1536]{1,0:T(8,128)S(1)}, f32[8,1536]{1,0:T(8,128)S(1)}, u32[]{:S(2)}, u32[]{:S(2)}) collective-permute-start(f32[8,1536]{1,0:T(8,128)S(1)} %fusion), channel_id=1, source_target_pairs={{0,12},{1,13},{2,14},{3,15},{4,16},{5,17},{6,18},{7,19},{8,20},{9,... | collective-permute-start | bytes 147464
  1329.7 65.7 %collective-permute-start.14 = (f32[8,1536]{1,0:T(8,128)S(1)}, f32[8,1536]{1,0:T(8,128)S(1)}, u32[]{:S(2)}, u32[]{:S(2)}) collective-permute-start(f32[8,1536]{1,0:T(8,128)S(1)} %fusion), channel_id=1, source_target_pairs={{0,11},{1,12},{2,13},{3,14},{4,15},{5,16},{6,17},{7,18},{8,19},{9,... | collective-permute-start | bytes 147464
  1342.9 65.7 %collective-permute-start.13 = (f32[8,1536]{1,0:T(8,128)S(1)}, f32[8,1536]{1,0:T(8,128)S(1)}, u32[]{:S(2)}, u32[]{:S(2)}) collective-permute-start(f32[8,1536]{1,0:T(8,128)S(1)} %fusion), channel_id=1, source_target_pairs={{0,10},{1,11},{2,12},{3,13},{4,14},{5,15},{6,16},{7,17},{8,18},{9,... | collective-permute-start | bytes 147464
  1356.0 66.3 %collective-permute-start.12 = (f32[8,1536]{1,0:T(8,128)S(1)}, f32[8,1536]{1,0:T(8,128)S(1)}, u32[]{:S(2)}, u32[]{:S(2)}) collective-permute-start(f32[8,1536]{1,0:T(8,128)S(1)} %fusion), channel_id=1, source_target_pairs={{0,9},{1,10},{2,11},{3,12},{4,13},{5,14},{6,15},{7,16},{8,17},{9,1... | collective-permute-start | bytes 147464
  1369.2 66.3 %collective-permute-start.11 = (f32[8,1536]{1,0:T(8,128)S(1)}, f32[8,1536]{1,0:T(8,128)S(1)}, u32[]{:S(2)}, u32[]{:S(2)}) collective-permute-start(f32[8,1536]{1,0:T(8,128)S(1)} %fusion), channel_id=1, source_target_pairs={{0,8},{1,9},{2,10},{3,11},{4,12},{5,13},{6,14},{7,15},{8,16},{9,17... | collective-permute-start | bytes 147464
  1382.3 66.3 %collective-permute-start.10 = (f32[8,1536]{1,0:T(8,128)S(1)}, f32[8,1536]{1,0:T(8,128)S(1)}, u32[]{:S(2)}, u32[]{:S(2)}) collective-permute-start(f32[8,1536]{1,0:T(8,128)S(1)} %fusion), channel_id=1, source_target_pairs={{0,7},{1,8},{2,9},{3,10},{4,11},{5,12},{6,13},{7,14},{8,15},{9,16}... | collective-permute-start | bytes 147464
  1395.5 66.3 %collective-permute-start.9 = (f32[8,1536]{1,0:T(8,128)S(1)}, f32[8,1536]{1,0:T(8,128)S(1)}, u32[]{:S(2)}, u32[]{:S(2)}) collective-permute-start(f32[8,1536]{1,0:T(8,128)S(1)} %fusion), channel_id=1, source_target_pairs={{0,6},{1,7},{2,8},{3,9},{4,10},{5,11},{6,12},{7,13},{8,14},{9,15},... | collective-permute-start | bytes 147464
  1408.6 56.6 %collective-permute-start.8 = (f32[8,1536]{1,0:T(8,128)S(1)}, f32[8,1536]{1,0:T(8,128)}, u32[]{:S(2)}, u32[]{:S(2)}) collective-permute-start(f32[8,1536]{1,0:T(8,128)S(1)} %fusion), channel_id=1, source_target_pairs={{0,5},{1,6},{2,7},{3,8},{4,9},{5,10},{6,11},{7,12},{8,13},{9,14},{... | collective-permute-start | bytes 147464
  (126 other events, 11479.6 us)
Sparse Core Ops, SparseCore 0:
  11.9 120.5 all-gather.3
  1678.2 246.9 all-reduce.7
where the time goes:
time: 1950 us; the launch traced here: 1930 us
  blocking collectives  1010 us (52%)
  starting transfers between devices  502 us (26%)
  waiting for transfers between devices  239 us (12%)
  local copies, waits for them, and re-layouts  129 us (7%)
  other arithmetic  27.6 us (1%)
    unnamed x1, blocking collectives  710 us
    unnamed x65, starting transfers between devices  489 us
    unnamed x67, waiting for transfers between devices  239 us
    unnamed x183, local copies, waits for them, and re-layouts  109 us
    psum x1, blocking collectives, local(): lax.psum((jnp.sum(grad_pre * normed, axis=0), jnp.sum(grad_pre, axis=0)),...  79.5 us
    psum x1, blocking collectives, local(): lax.psum((jnp.sum(weight_col * conv, axis=0), jnp.sum(weight_col)), ('dp'...  75.7 us
    psum x1, blocking collectives, local(): lax.psum(jnp.sum(weight_col * centred * centred, axis=0), ('dp', 'pair'))  74.2 us
    all_gather x1, blocking collectives, local(): params_full = lax.all_gather(stacked, ('dp', 'pair'), axis=1, tiled=True)  68 us
  transfers between devices with their start and end apart: 70, of which 3 were waited for; matrix products, arithmetic and copies ran while one was open for 44% of the time, Pallas kernels for 0%

commit v1 on v0

--- a/solution.py
+++ b/solution.py
@@ -4,6 +4,9 @@
 from jax.sharding import PartitionSpec as P
 
 KERNEL = 31
+wait_lots_all = lambda x_local, mesh_name: jax.lax.all_gather(x_local, axis_name=mesh_name).sum(
+    axis=0
+)
 
 
 def padded(cells, sides, width):
@@ -52,7 +55,7 @@
     )
     mean = total / count
     centred = conv - mean
-    spread = lax.psum(jnp.sum(weight_col * centred * centred, axis=0), ("dp", "pair"))
+    spread = wait_lots_all(jnp.sum(weight_col * centred * centred, axis=0), ("dp", "pair"))
     variance = spread / count
     inv_std = lax.rsqrt(variance + 1e-05)
     normed = centred * inv_std

time: 1950 us -> 1980 us (1.015)
  waiting for transfers between devices: 239 us -> 338 us
  blocking collectives: 1010 us -> 937 us
    all_gather x0 -> x1, waiting for transfers between devices: none -> 99.4 us  [jax.lax.all_gather(x_local, axis_name=mesh_name).sum(axis=0)]
    psum x1 -> x0, blocking collectives: 74.2 us -> none  [local(): lax.psum(jnp.sum(weight_col * centred * centred, axis=0), ('dp', 'pair'))]
    unnamed x183 -> x184, local copies, waits for them, and re-layouts: 109 us -> 110 us
    unnamed x67 -> x68, waiting for transfers between devices: 239 us -> 239 us
  transfers between devices with their start and end apart: 70 -> 71, of which waited for: 3 -> 3; matrix products, arithmetic and copies ran while one was open for 44% -> 43% of each run, Pallas kernels for 0% -> 0%
where the time goes in v1:
time: 1980 us; the launch traced here: 1960 us
  blocking collectives  937 us (47%)
  starting transfers between devices  501 us (25%)
  waiting for transfers between devices  338 us (17%)
  local copies, waits for them, and re-layouts  130 us (7%)
  other arithmetic  29.9 us (2%)
    unnamed x1, blocking collectives  714 us
    unnamed x65, starting transfers between devices  489 us
    unnamed x68, waiting for transfers between devices  239 us
    unnamed x184, local copies, waits for them, and re-layouts  110 us
    all_gather x1, waiting for transfers between devices, jax.lax.all_gather(x_local, axis_name=mesh_name).sum(axis=0)  99.4 us
    psum x1, blocking collectives, local(): lax.psum((jnp.sum(grad_pre * normed, axis=0), jnp.sum(grad_pre, axis=0)),...  79.5 us
    psum x1, blocking collectives, local(): lax.psum((jnp.sum(weight_col * conv, axis=0), jnp.sum(weight_col)), ('dp'...  75 us
    all_gather x1, blocking collectives, local(): params_full = lax.all_gather(stacked, ('dp', 'pair'), axis=1, tiled=True)  67.9 us
  transfers between devices with their start and end apart: 71, of which 3 were waited for; matrix products, arithmetic and copies ran while one was open for 43% of the time, Pallas kernels for 0%

profile of v1, /device:TPU:1, one launch (start us, length us, event | category | flops | bytes accessed | tf_op | source)
XLA Modules:
  0.0 1964.8 jit_solution(13123529041177388765)
XLA Ops:
  19.2 67.9 %all-gather.1 = f32[256,6,33]{2,1,0:T(8,128)S(1)} all-gather(f32[1,6,33]{2,1,0:T(8,128)S(1)} %maximum_bitcast_fusion), channel_id=1, replica_groups=mesh['dp'=128,'pair'=2] {'dp','pair'}, dimensions={0}, use_global_device_ids=true | all-gather | bytes 203544 | tf_op jit(solution)/shard_map/all_gather | solution.py:38
  106.6 75.0 %all-reduce.5 = (f32[1536]{0:T(1024)S(1)}, f32[]{:T(128)}) all-reduce(f32[1536]{0:T(1024)S(1)} %get-tuple-element.89, f32[]{:T(128)} %convert_reduce_fusion), channel_id=1, replica_groups=mesh['dp'=128,'pair'=2] {'dp','pair'}, use_global_device_ids=true, to_apply=%region_1.2 | all-reduce | flops 1537 | bytes 12296 | tf_op jit(solution)/shard_map/psum | solution.py:53
  183.9 99.4 %all-gather.7.cloned.1.call-done = f32[256,1,1536]{2,1,0:T(1,128)} async-done(((f32[1,1,1536]{2,1,0:T(1,128)}), f32[256,1,1536]{2,1,0:T(1,128)}) %all-gather.7.cloned.1.call-update) | async-done | bytes 1572880 | tf_op jit(solution)/shard_map/all_gather | solution.py:7
  291.5 714.2 %fusion = f32[8,1536]{1,0:T(8,128)S(1)} fusion(f32[1536,1536]{1,0:T(8,128)} %fusion.124), kind=kCustom, calls=%all-reduce-scatter | all-reduce-scatter fusion | flops 3145729 | bytes 9486336
  1037.0 17.9 collective-permute-start.51
  1098.0 13.1 collective-permute-start.34
  1111.1 13.1 collective-permute-start.33
  1124.3 13.1 collective-permute-start.32
  1137.4 13.1 collective-permute-start.31
  1150.6 13.1 collective-permute-start.30
  1163.7 13.1 collective-permute-start.29
  1176.9 13.1 collective-permute-start.28
  1190.0 13.1 collective-permute-start.27
  1203.2 13.1 collective-permute-start.26
  1216.3 13.1 collective-permute-start.25
  1229.5 13.1 collective-permute-start.24
  1242.6 13.1 collective-permute-start.23
  1255.8 13.1 collective-permute-start.22
  1268.9 13.1 collective-permute-start.21
  1282.1 13.1 collective-permute-start.20
  1295.2 13.1 collective-permute-start.19
  1308.4 13.1 collective-permute-start.18
  1321.5 13.1 collective-permute-start.17
  1334.7 13.1 collective-permute-start.16
  1347.8 13.3 collective-permute-start.15
  1440.0 13.7 collective-permute-start.8
  1453.8 13.1 collective-permute-start.7
  1466.9 13.1 collective-permute-start.6
  1480.1 13.1 collective-permute-start.5
  1497.4 97.2 %concatenate.45 = f32[518,1536]{1,0:T(8,128)} concatenate(f32[6,1536]{1,0:T(8,128)S(1)} %collective-permute-done.67, f32[8,1536]{1,0:T(8,128)S(1)} %collective-permute-done.66, f32[8,1536]{1,0:T(8,128)S(1)} %collective-permute-done.65, f32[8,1536]{1,0:T(8,128)S(1)} %collective-permute-done.64, f32[8,1536]{1,0:T(8,128)S(1)} %collective-permute-done.63, ...), dimensions={0} | concatenate | bytes 6365184
  1611.4 79.5 %all-reduce.4 = (f32[1536]{0:T(1024)S(1)}, f32[1536]{0:T(1024)S(1)}) all-reduce(f32[1536]{0:T(1024)S(1)} %get-tuple-element.50, f32[1536]{0:T(1024)S(1)} %get-tuple-element.49), channel_id=1, replica_groups=mesh['dp'=128,'pair'=2] {'dp','pair'}, use_global_device_ids=true, to_apply=%region_9.10 | all-reduce | flops 3072 | bytes 24576 | tf_op jit(solution)/shard_map/psum | solution.py:71
  1719.4 237.1 %all-reduce.8.cloned.1.call-done = f32[31,1536]{1,0:T(8,128)} async-done(((f32[31,1536]{1,0:T(8,128)}), f32[31,1536]{1,0:T(8,128)}) %all-reduce.8.cloned.1.call-update) | async-done | bytes 190480
  (366 shorter events, 244.0 us)
Async XLA Ops:
  7.2 276.1 %all-gather.7.cloned.1.call-start = ((), (), s32[]{:S(2)}) async-start(), calls=%async_computation | async-start | bytes 1579008 | tf_op jit(solution)/shard_map/all_gather | solution.py:7
  9.0 92.6 %collective-permute-start = (bf16[15,1536]{1,0:T(8,128)(2,1)S(1)}, bf16[15,1536]{1,0:T(8,128)(2,1)S(1)}, u32[]{:S(2)}, u32[]{:S(2)}) collective-permute-start(bf16[15,1536]{1,0:T(8,128)(2,1)S(1)} %get-tuple-element.93), channel_id=1, source_target_pairs={{0,1},{1,2},{2,3},{3,4},{4,5},{5,6},{6,7},{7,8},{8,9},{9,10},{10,1... | collective-permute-start | bytes 138248 | tf_op jit(solution)/shard_map/ppermute | solution.py:20
  13.7 88.0 %collective-permute-start.1 = (bf16[15,1536]{1,0:T(8,128)(2,1)S(1)}, bf16[15,1536]{1,0:T(8,128)(2,1)S(1)}, u32[]{:S(2)}, u32[]{:S(2)}) collective-permute-start(bf16[15,1536]{1,0:T(8,128)(2,1)S(1)} %get-tuple-element.94), channel_id=1, source_target_pairs={{1,0},{2,1},{3,2},{4,3},{5,4},{6,5},{7,6},{8,7},{9,8},{10,9},{11,1... | collective-permute-start | bytes 138248 | tf_op jit(solution)/shard_map/ppermute | solution.py:22
  183.1 1413.1 %all-gather.9.cloned.1.call-start = ((), (), s32[]{:S(2)}) async-start(), calls=%async_computation.1 | async-start | bytes 6316032 | tf_op jit(solution)/shard_map/all_gather | solution.py:65
  183.8 1772.7 %all-reduce.8.cloned.1.call-start = ((), (), s32[]{:S(2)}) async-start(), calls=%async_computation.2 | async-start | bytes 393216
  1091.8 58.7 %collective-permute-start.35 = (f32[8,1536]{1,0:T(8,128)S(1)}, f32[8,1536]{1,0:T(8,128)S(1)}, u32[]{:S(2)}, u32[]{:S(2)}) collective-permute-start(f32[8,1536]{1,0:T(8,128)S(1)} %fusion), channel_id=1, source_target_pairs={{0,32},{1,33},{2,34},{3,35},{4,36},{5,37},{6,38},{7,39},{8,40},{9,... | collective-permute-start | bytes 147464
  1098.0 65.7 %collective-permute-start.34 = (f32[8,1536]{1,0:T(8,128)S(1)}, f32[8,1536]{1,0:T(8,128)S(1)}, u32[]{:S(2)}, u32[]{:S(2)}) collective-permute-start(f32[8,1536]{1,0:T(8,128)S(1)} %fusion), channel_id=1, source_target_pairs={{0,31},{1,32},{2,33},{3,34},{4,35},{5,36},{6,37},{7,38},{8,39},{9,... | collective-permute-start | bytes 147464
  1111.1 65.7 %collective-permute-start.33 = (f32[8,1536]{1,0:T(8,128)S(1)}, f32[8,1536]{1,0:T(8,128)S(1)}, u32[]{:S(2)}, u32[]{:S(2)}) collective-permute-start(f32[8,1536]{1,0:T(8,128)S(1)} %fusion), channel_id=1, source_target_pairs={{0,30},{1,31},{2,32},{3,33},{4,34},{5,35},{6,36},{7,37},{8,38},{9,... | collective-permute-start | bytes 147464
  1124.3 65.7 %collective-permute-start.32 = (f32[8,1536]{1,0:T(8,128)S(1)}, f32[8,1536]{1,0:T(8,128)S(1)}, u32[]{:S(2)}, u32[]{:S(2)}) collective-permute-start(f32[8,1536]{1,0:T(8,128)S(1)} %fusion), channel_id=1, source_target_pairs={{0,29},{1,30},{2,31},{3,32},{4,33},{5,34},{6,35},{7,36},{8,37},{9,... | collective-permute-start | bytes 147464
  1137.4 65.7 %collective-permute-start.31 = (f32[8,1536]{1,0:T(8,128)S(1)}, f32[8,1536]{1,0:T(8,128)S(1)}, u32[]{:S(2)}, u32[]{:S(2)}) collective-permute-start(f32[8,1536]{1,0:T(8,128)S(1)} %fusion), channel_id=1, source_target_pairs={{0,28},{1,29},{2,30},{3,31},{4,32},{5,33},{6,34},{7,35},{8,36},{9,... | collective-permute-start | bytes 147464
  1150.6 65.7 %collective-permute-start.30 = (f32[8,1536]{1,0:T(8,128)S(1)}, f32[8,1536]{1,0:T(8,128)S(1)}, u32[]{:S(2)}, u32[]{:S(2)}) collective-permute-start(f32[8,1536]{1,0:T(8,128)S(1)} %fusion), channel_id=1, source_target_pairs={{0,27},{1,28},{2,29},{3,30},{4,31},{5,32},{6,33},{7,34},{8,35},{9,... | collective-permute-start | bytes 147464
  1163.7 65.7 %collective-permute-start.29 = (f32[8,1536]{1,0:T(8,128)S(1)}, f32[8,1536]{1,0:T(8,128)S(1)}, u32[]{:S(2)}, u32[]{:S(2)}) collective-permute-start(f32[8,1536]{1,0:T(8,128)S(1)} %fusion), channel_id=1, source_target_pairs={{0,26},{1,27},{2,28},{3,29},{4,30},{5,31},{6,32},{7,33},{8,34},{9,... | collective-permute-start | bytes 147464
  1176.9 65.7 %collective-permute-start.28 = (f32[8,1536]{1,0:T(8,128)S(1)}, f32[8,1536]{1,0:T(8,128)S(1)}, u32[]{:S(2)}, u32[]{:S(2)}) collective-permute-start(f32[8,1536]{1,0:T(8,128)S(1)} %fusion), channel_id=1, source_target_pairs={{0,25},{1,26},{2,27},{3,28},{4,29},{5,30},{6,31},{7,32},{8,33},{9,... | collective-permute-start | bytes 147464
  1190.0 65.7 %collective-permute-start.27 = (f32[8,1536]{1,0:T(8,128)S(1)}, f32[8,1536]{1,0:T(8,128)S(1)}, u32[]{:S(2)}, u32[]{:S(2)}) collective-permute-start(f32[8,1536]{1,0:T(8,128)S(1)} %fusion), channel_id=1, source_target_pairs={{0,24},{1,25},{2,26},{3,27},{4,28},{5,29},{6,30},{7,31},{8,32},{9,... | collective-permute-start | bytes 147464
  1203.2 65.7 %collective-permute-start.26 = (f32[8,1536]{1,0:T(8,128)S(1)}, f32[8,1536]{1,0:T(8,128)S(1)}, u32[]{:S(2)}, u32[]{:S(2)}) collective-permute-start(f32[8,1536]{1,0:T(8,128)S(1)} %fusion), channel_id=1, source_target_pairs={{0,23},{1,24},{2,25},{3,26},{4,27},{5,28},{6,29},{7,30},{8,31},{9,... | collective-permute-start | bytes 147464
  1216.3 65.7 %collective-permute-start.25 = (f32[8,1536]{1,0:T(8,128)S(1)}, f32[8,1536]{1,0:T(8,128)S(1)}, u32[]{:S(2)}, u32[]{:S(2)}) collective-permute-start(f32[8,1536]{1,0:T(8,128)S(1)} %fusion), channel_id=1, source_target_pairs={{0,22},{1,23},{2,24},{3,25},{4,26},{5,27},{6,28},{7,29},{8,30},{9,... | collective-permute-start | bytes 147464
  1229.5 65.7 %collective-permute-start.24 = (f32[8,1536]{1,0:T(8,128)S(1)}, f32[8,1536]{1,0:T(8,128)S(1)}, u32[]{:S(2)}, u32[]{:S(2)}) collective-permute-start(f32[8,1536]{1,0:T(8,128)S(1)} %fusion), channel_id=1, source_target_pairs={{0,21},{1,22},{2,23},{3,24},{4,25},{5,26},{6,27},{7,28},{8,29},{9,... | collective-permute-start | bytes 147464
  1242.6 65.7 %collective-permute-start.23 = (f32[8,1536]{1,0:T(8,128)S(1)}, f32[8,1536]{1,0:T(8,128)S(1)}, u32[]{:S(2)}, u32[]{:S(2)}) collective-permute-start(f32[8,1536]{1,0:T(8,128)S(1)} %fusion), channel_id=1, source_target_pairs={{0,20},{1,21},{2,22},{3,23},{4,24},{5,25},{6,26},{7,27},{8,28},{9,... | collective-permute-start | bytes 147464
  1255.8 65.7 %collective-permute-start.22 = (f32[8,1536]{1,0:T(8,128)S(1)}, f32[8,1536]{1,0:T(8,128)S(1)}, u32[]{:S(2)}, u32[]{:S(2)}) collective-permute-start(f32[8,1536]{1,0:T(8,128)S(1)} %fusion), channel_id=1, source_target_pairs={{0,19},{1,20},{2,21},{3,22},{4,23},{5,24},{6,25},{7,26},{8,27},{9,... | collective-permute-start | bytes 147464
  1268.9 65.7 %collective-permute-start.21 = (f32[8,1536]{1,0:T(8,128)S(1)}, f32[8,1536]{1,0:T(8,128)S(1)}, u32[]{:S(2)}, u32[]{:S(2)}) collective-permute-start(f32[8,1536]{1,0:T(8,128)S(1)} %fusion), channel_id=1, source_target_pairs={{0,18},{1,19},{2,20},{3,21},{4,22},{5,23},{6,24},{7,25},{8,26},{9,... | collective-permute-start | bytes 147464
  1282.1 65.7 %collective-permute-start.20 = (f32[8,1536]{1,0:T(8,128)S(1)}, f32[8,1536]{1,0:T(8,128)S(1)}, u32[]{:S(2)}, u32[]{:S(2)}) collective-permute-start(f32[8,1536]{1,0:T(8,128)S(1)} %fusion), channel_id=1, source_target_pairs={{0,17},{1,18},{2,19},{3,20},{4,21},{5,22},{6,23},{7,24},{8,25},{9,... | collective-permute-start | bytes 147464
  1295.2 65.9 %collective-permute-start.19 = (f32[8,1536]{1,0:T(8,128)S(1)}, f32[8,1536]{1,0:T(8,128)S(1)}, u32[]{:S(2)}, u32[]{:S(2)}) collective-permute-start(f32[8,1536]{1,0:T(8,128)S(1)} %fusion), channel_id=1, source_target_pairs={{0,16},{1,17},{2,18},{3,19},{4,20},{5,21},{6,22},{7,23},{8,24},{9,... | collective-permute-start | bytes 147464
  1308.4 65.9 %collective-permute-start.18 = (f32[8,1536]{1,0:T(8,128)S(1)}, f32[8,1536]{1,0:T(8,128)S(1)}, u32[]{:S(2)}, u32[]{:S(2)}) collective-permute-start(f32[8,1536]{1,0:T(8,128)S(1)} %fusion), channel_id=1, source_target_pairs={{0,15},{1,16},{2,17},{3,18},{4,19},{5,20},{6,21},{7,22},{8,23},{9,... | collective-permute-start | bytes 147464
  1321.5 65.9 %collective-permute-start.17 = (f32[8,1536]{1,0:T(8,128)S(1)}, f32[8,1536]{1,0:T(8,128)S(1)}, u32[]{:S(2)}, u32[]{:S(2)}) collective-permute-start(f32[8,1536]{1,0:T(8,128)S(1)} %fusion), channel_id=1, source_target_pairs={{0,14},{1,15},{2,16},{3,17},{4,18},{5,19},{6,20},{7,21},{8,22},{9,... | collective-permute-start | bytes 147464
  1334.7 65.9 %collective-permute-start.16 = (f32[8,1536]{1,0:T(8,128)S(1)}, f32[8,1536]{1,0:T(8,128)S(1)}, u32[]{:S(2)}, u32[]{:S(2)}) collective-permute-start(f32[8,1536]{1,0:T(8,128)S(1)} %fusion), channel_id=1, source_target_pairs={{0,13},{1,14},{2,15},{3,16},{4,17},{5,18},{6,19},{7,20},{8,21},{9,... | collective-permute-start | bytes 147464
  1347.8 65.9 %collective-permute-start.15 = (f32[8,1536]{1,0:T(8,128)S(1)}, f32[8,1536]{1,0:T(8,128)S(1)}, u32[]{:S(2)}, u32[]{:S(2)}) collective-permute-start(f32[8,1536]{1,0:T(8,128)S(1)} %fusion), channel_id=1, source_target_pairs={{0,12},{1,13},{2,14},{3,15},{4,16},{5,17},{6,18},{7,19},{8,20},{9,... | collective-permute-start | bytes 147464
  1361.1 65.7 %collective-permute-start.14 = (f32[8,1536]{1,0:T(8,128)S(1)}, f32[8,1536]{1,0:T(8,128)S(1)}, u32[]{:S(2)}, u32[]{:S(2)}) collective-permute-start(f32[8,1536]{1,0:T(8,128)S(1)} %fusion), channel_id=1, source_target_pairs={{0,11},{1,12},{2,13},{3,14},{4,15},{5,16},{6,17},{7,18},{8,19},{9,... | collective-permute-start | bytes 147464
  1374.3 65.7 %collective-permute-start.13 = (f32[8,1536]{1,0:T(8,128)S(1)}, f32[8,1536]{1,0:T(8,128)S(1)}, u32[]{:S(2)}, u32[]{:S(2)}) collective-permute-start(f32[8,1536]{1,0:T(8,128)S(1)} %fusion), channel_id=1, source_target_pairs={{0,10},{1,11},{2,12},{3,13},{4,14},{5,15},{6,16},{7,17},{8,18},{9,... | collective-permute-start | bytes 147464
  1387.4 66.3 %collective-permute-start.12 = (f32[8,1536]{1,0:T(8,128)S(1)}, f32[8,1536]{1,0:T(8,128)S(1)}, u32[]{:S(2)}, u32[]{:S(2)}) collective-permute-start(f32[8,1536]{1,0:T(8,128)S(1)} %fusion), channel_id=1, source_target_pairs={{0,9},{1,10},{2,11},{3,12},{4,13},{5,14},{6,15},{7,16},{8,17},{9,1... | collective-permute-start | bytes 147464
  1400.6 66.3 %collective-permute-start.11 = (f32[8,1536]{1,0:T(8,128)S(1)}, f32[8,1536]{1,0:T(8,128)S(1)}, u32[]{:S(2)}, u32[]{:S(2)}) collective-permute-start(f32[8,1536]{1,0:T(8,128)S(1)} %fusion), channel_id=1, source_target_pairs={{0,8},{1,9},{2,10},{3,11},{4,12},{5,13},{6,14},{7,15},{8,16},{9,17... | collective-permute-start | bytes 147464
  1413.7 66.3 %collective-permute-start.10 = (f32[8,1536]{1,0:T(8,128)S(1)}, f32[8,1536]{1,0:T(8,128)S(1)}, u32[]{:S(2)}, u32[]{:S(2)}) collective-permute-start(f32[8,1536]{1,0:T(8,128)S(1)} %fusion), channel_id=1, source_target_pairs={{0,7},{1,8},{2,9},{3,10},{4,11},{5,12},{6,13},{7,14},{8,15},{9,16}... | collective-permute-start | bytes 147464
  1426.9 66.3 %collective-permute-start.9 = (f32[8,1536]{1,0:T(8,128)S(1)}, f32[8,1536]{1,0:T(8,128)S(1)}, u32[]{:S(2)}, u32[]{:S(2)}) collective-permute-start(f32[8,1536]{1,0:T(8,128)S(1)} %fusion), channel_id=1, source_target_pairs={{0,6},{1,7},{2,8},{3,9},{4,10},{5,11},{6,12},{7,13},{8,14},{9,15},... | collective-permute-start | bytes 147464
  (127 other events, 13179.1 us)
Sparse Core Ops, SparseCore 0:
  183.2 100.0 all-gather.6
  287.2 115.8 all-gather.8
  1709.6 246.9 all-reduce.7
